TPU v7x, 32 devices: a whole 2x2x4 slice. The times are simulated.
32 devices in a mesh: grp: 4 (over y, x), seq: 8 (over z, core).
Axes of the slice: x: 2, y: 2, z: 4, core: 2. Of those that a mesh axis runs over, the one named last changes fastest.
Arguments:
- queries: bfloat16 [4096, 1280], P(('grp', 'seq')), may hold values from -6 to 6
- image_keys: bfloat16 [4096, 1280], P(('grp', 'seq')), may hold values from -6 to 6
- image_values: bfloat16 [4096, 1280], P(('grp', 'seq')), may hold values from -6 to 6
- out_grad: bfloat16 [4096, 1280], P(('grp', 'seq')), may hold values from -6 to 6
- text_keys: bfloat16 [256, 1280], P('seq'), may hold values from -6 to 6
- text_values: bfloat16 [256, 1280], P('seq'), may hold values from -6 to 6
- reward_ranks: int32 [4], replicated, may hold values from 0 to 3, each once
Outputs:
- grad_queries: bfloat16 [4096, 1280], P(('grp', 'seq'))
- grad_keys: bfloat16 [4096, 1280], P(('grp', 'seq'))
- grad_values: bfloat16 [4096, 1280], P(('grp', 'seq'))
- grad_text_keys: bfloat16 [256, 1280], P('seq')
- grad_text_values: bfloat16 [256, 1280], P('seq')
Inputs may be any that keep to these rules, and one draw needn't show every extreme that they name: `reward_ranks`: each of the 4 ranks appears once.
All inputs are finite; a program needn't handle non-finite values.
Results may differ from a plain program's by a relative error of at most 0.012.
Values may be sent and summed in bfloat16 or wider, within the bound.
A program may use at most 192 MiB of HBM per device.

v0:
```python
import math

import jax
import jax.numpy as jnp
from jax import lax
from jax.sharding import PartitionSpec as P

HEADS = 20
HEAD_DIM = 64


def split_heads(matrix):
    return matrix.reshape(matrix.shape[0], HEADS, HEAD_DIM)


def block_size(rows):
    return math.gcd(rows, 512)


def absorb_block(running, key_rows, value_rows, query_heads, cotan_heads):
    score_scale = HEAD_DIM ** (-0.5)
    highest, summed_weights, weighted_sum = running
    key_heads = split_heads(key_rows)
    value_heads = split_heads(value_rows)
    scores = score_scale * jnp.einsum(
        "qhe,khe->hqk", query_heads, key_heads, preferred_element_type=jnp.float32
    )
    products = jnp.einsum(
        "qhe,khe->hqk", cotan_heads, value_heads, preferred_element_type=jnp.float32
    )
    new_high = jnp.maximum(highest, jnp.max(scores, -1))
    shrink = jnp.exp(highest - new_high)
    weights = jnp.exp(scores - new_high[..., None])
    summed_weights = summed_weights * shrink + jnp.sum(weights, -1)
    weighted_sum = weighted_sum * shrink + jnp.sum(weights * products, -1)
    return (new_high, summed_weights, weighted_sum)


def absorb(running, key_rows, value_rows, query_heads, cotan_heads):
    rows = key_rows.shape[0]
    width = block_size(rows)
    count = rows // width

    def absorb_one(state, pair):
        return (absorb_block(state, pair[0], pair[1], query_heads, cotan_heads), None)

    running, unused = lax.scan(
        absorb_one,
        running,
        (key_rows.reshape(count, width, -1), value_rows.reshape(count, width, -1)),
    )
    return running


def query_block_terms(running, key_rows, value_rows, query_heads, cotan_heads, log_total):
    score_scale = HEAD_DIM ** (-0.5)
    first_sum, second_sum = running
    key_heads = split_heads(key_rows)
    value_heads = split_heads(value_rows)
    scores = score_scale * jnp.einsum(
        "qhe,khe->hqk", query_heads, key_heads, preferred_element_type=jnp.float32
    )
    probabilities = jnp.exp(scores - log_total[..., None])
    products = jnp.einsum(
        "qhe,khe->hqk", cotan_heads, value_heads, preferred_element_type=jnp.float32
    )
    first_sum = first_sum + jnp.einsum(
        "hqk,khe->hqe",
        (probabilities * products).astype(jnp.bfloat16),
        key_heads,
        preferred_element_type=jnp.float32,
    )
    second_sum = second_sum + jnp.einsum(
        "hqk,khe->hqe",
        probabilities.astype(jnp.bfloat16),
        key_heads,
        preferred_element_type=jnp.float32,
    )
    return (first_sum, second_sum)


def query_terms(running, key_rows, value_rows, query_heads, cotan_heads, log_total):
    rows = key_rows.shape[0]
    width = block_size(rows)
    count = rows // width

    def query_one(state, pair):
        return (
            query_block_terms(state, pair[0], pair[1], query_heads, cotan_heads, log_total),
            None,
        )

    running, unused = lax.scan(
        query_one,
        running,
        (key_rows.reshape(count, width, -1), value_rows.reshape(count, width, -1)),
    )
    return running


def key_block_terms(query_heads, cotan_heads, log_total, grad_dot, key_rows, value_rows):
    score_scale = HEAD_DIM ** (-0.5)
    key_heads = split_heads(key_rows)
    value_heads = split_heads(value_rows)
    scores = score_scale * jnp.einsum(
        "qhe,khe->hqk", query_heads, key_heads, preferred_element_type=jnp.float32
    )
    probabilities = jnp.exp(scores - log_total[..., None])
    products = jnp.einsum(
        "qhe,khe->hqk", cotan_heads, value_heads, preferred_element_type=jnp.float32
    )
    slopes = (probabilities * (products - grad_dot[..., None])).astype(jnp.bfloat16)
    key_grads = score_scale * jnp.einsum(
        "hqk,qhe->khe", slopes, query_heads, preferred_element_type=jnp.float32
    )
    value_grads = jnp.einsum(
        "hqk,qhe->khe",
        probabilities.astype(jnp.bfloat16),
        cotan_heads,
        preferred_element_type=jnp.float32,
    )
    return (key_grads.reshape(key_rows.shape[0], -1), value_grads.reshape(key_rows.shape[0], -1))


def key_terms(query_heads, cotan_heads, log_total, grad_dot, key_rows, value_rows):
    rows = query_heads.shape[0]
    width = block_size(rows)
    count = rows // width
    heads_count = log_total.shape[0]
    zero_grads = jnp.zeros((key_rows.shape[0], key_rows.shape[1]), jnp.float32)
    log_blocks = jnp.transpose(log_total.reshape(heads_count, count, width), (1, 0, 2))
    dot_blocks = jnp.transpose(grad_dot.reshape(heads_count, count, width), (1, 0, 2))

    def key_one(state, group):
        key_grads, value_grads = key_block_terms(
            group[0], group[1], group[2], group[3], key_rows, value_rows
        )
        return ((state[0] + key_grads, state[1] + value_grads), None)

    totals, unused = lax.scan(
        key_one,
        (zero_grads, zero_grads),
        (
            query_heads.reshape(count, width, HEADS, HEAD_DIM),
            cotan_heads.reshape(count, width, HEADS, HEAD_DIM),
            log_blocks,
            dot_blocks,
        ),
    )
    return totals


def local(queries, image_keys, image_values, out_grad, text_keys, text_values, reward_ranks):
    row_count = queries.shape[0]
    features = queries.shape[1]
    images_count = reward_ranks.shape[0]
    picked = jnp.sum(
        jnp.where(jnp.arange(images_count) == lax.axis_index("grp"), reward_ranks, 0)
    ).astype(jnp.float32)
    advantage = (picked - 0.5 * (images_count - 1)) / math.sqrt(
        (images_count * images_count - 1) / 12.0
    )
    cotangent = (advantage * out_grad.astype(jnp.float32)).astype(jnp.bfloat16)
    query_heads = split_heads(queries)
    cotan_heads = split_heads(cotangent)
    flat_zero = jnp.zeros((HEADS, row_count), jnp.float32)
    wide_zero = jnp.zeros((HEADS, row_count, HEAD_DIM), jnp.float32)
    start_state = (jnp.full((HEADS, row_count), -1e30, jnp.float32), flat_zero, flat_zero)
    whole_text = (
        lax.all_gather(text_keys, "seq", axis=0, tiled=True),
        lax.all_gather(text_values, "seq", axis=0, tiled=True),
    )
    running = absorb(start_state, whole_text[0], whole_text[1], query_heads, cotan_heads)
    pieces = (
        lax.all_gather(image_keys, "seq", axis=0, tiled=True),
        lax.all_gather(image_values, "seq", axis=0, tiled=True),
    )
    running = absorb(running, pieces[0], pieces[1], query_heads, cotan_heads)
    highest, summed_weights, weighted_sum = running
    log_total = highest + jnp.log(summed_weights)
    grad_dot = weighted_sum / summed_weights
    text_state = query_terms(
        (wide_zero, wide_zero), whole_text[0], whole_text[1], query_heads, cotan_heads, log_total
    )
    pieces = (
        lax.all_gather(image_keys, "seq", axis=0, tiled=True),
        lax.all_gather(image_values, "seq", axis=0, tiled=True),
    )
    first_sum, second_sum = query_terms(
        text_state, pieces[0], pieces[1], query_heads, cotan_heads, log_total
    )
    grad_query = HEAD_DIM ** (-0.5) * (first_sum - grad_dot[..., None] * second_sum)
    grad_queries = (
        jnp.transpose(grad_query, (1, 0, 2)).reshape(row_count, features).astype(jnp.bfloat16)
    )
    all_logs, all_dots = (
        lax.all_gather(log_total.T, "seq", axis=0, tiled=True),
        lax.all_gather(grad_dot.T, "seq", axis=0, tiled=True),
    )
    pieces = (
        lax.all_gather(queries, "seq", axis=0, tiled=True),
        lax.all_gather(cotangent, "seq", axis=0, tiled=True),
    )
    visiting_queries = split_heads(pieces[0])
    visiting_cotans = split_heads(pieces[1])
    key_grads, value_grads = key_terms(
        visiting_queries, visiting_cotans, all_logs.T, all_dots.T, image_keys, image_values
    )
    grad_keys = key_grads.astype(jnp.bfloat16)
    grad_values = value_grads.astype(jnp.bfloat16)
    text_key_part, text_value_part = key_terms(
        query_heads, cotan_heads, log_total, grad_dot, whole_text[0], whole_text[1]
    )
    summed = lax.psum((text_key_part, text_value_part), ("grp", "seq"))
    owned_rows = text_keys.shape[0]
    offset = lax.axis_index("seq") * owned_rows
    text_key_sum = lax.dynamic_slice_in_dim(summed[0], offset, owned_rows, 0)
    text_value_sum = lax.dynamic_slice_in_dim(summed[1], offset, owned_rows, 0)
    return (
        grad_queries,
        grad_keys,
        grad_values,
        text_key_sum.astype(jnp.bfloat16),
        text_value_sum.astype(jnp.bfloat16),
    )


def solution(mesh):
    in_specs = (
        P(("grp", "seq"), None),
        P(("grp", "seq"), None),
        P(("grp", "seq"), None),
        P(("grp", "seq"), None),
        P("seq", None),
        P("seq", None),
        P(),
    )
    out_specs = (
        P(("grp", "seq"), None),
        P(("grp", "seq"), None),
        P(("grp", "seq"), None),
        P("seq", None),
        P("seq", None),
    )
    return jax.shard_map(local, mesh=mesh, in_specs=in_specs, out_specs=out_specs, check_vma=False)
```

profile of v0, /device:TPU:0, one launch (start us, length us, event | category | flops | bytes accessed | tf_op | source)
XLA Modules:
  0.0 309.3 jit_solution(9501819882001800209)
XLA Ops:
  15.5 20.7 %all_gather.26 = bf16[256,1280]{1,0:T(8,128)(2,1)S(1)} all-gather(bf16[32,1280]{1,0:T(8,128)(2,1)S(1)} %copy-done.12), channel_id=1, replica_groups=mesh['grp'=4,'seq'=8] {'seq'}, dimensions={0}, use_global_device_ids=true | all-gather | bytes 737280 | tf_op jit(solution)/shard_map/all_gather | solution.py:170
  37.3 1.8 multiply_reduce_fusion.1
  39.1 18.8 %all_gather.27 = bf16[256,1280]{1,0:T(8,128)(2,1)} all-gather(bf16[32,1280]{1,0:T(8,128)(2,1)S(1)} %copy-done.13), channel_id=1, replica_groups=mesh['grp'=4,'seq'=8] {'seq'}, dimensions={0}, use_global_device_ids=true | all-gather | bytes 737280 | tf_op jit(solution)/shard_map/all_gather | solution.py:171
  57.9 2.2 copy.47
  60.1 3.5 %multiply_reduce_fusion = (f32[20,128]{1,0:T(8,128)S(1)}, f32[20,128]{1,0:T(8,128)S(1)}, f32[20,128,256]{2,1,0:T(8,128)}) fusion(f32[20,128,256]{2,1,0:T(8,128)S(1)} %get-tuple-element.398, f32[20,128]{1,0:T(8,128)S(1)} %broadcast_maximum_fusion, bf16[128,20,64]{0,2,1:T(8,128)(2,1)S(1)} %bitcast.159, bf16[256,20,64]{0,2,1:T(8,128)(2,1)} %bitcast.171), kind=kOutput, calls=%fused_computation.59 | convolution fusion | flops 87157760 | bytes 6256640 | tf_op jit(solution)/shard_map/while/body/eval_jaxpr/qhe,khe->hqk/dot_general | solution.py:28
  63.7 4.6 %copy.48 = bf16[2,512,1280]{1,2,0:T(8,128)(2,1)} copy(bf16[2,512,1280]{2,1,0:T(8,128)(2,1)} %bitcast.169) | data formatting | bytes 5242880 | tf_op jit(solution)/shard_map/while | solution.py:47
  68.3 20.9 %all-gather.7.cloned.1.call-done = bf16[1024,1280]{1,0:T(8,128)(2,1)} async-done(((bf16[128,1280]{1,0:T(8,128)(2,1)}), bf16[1024,1280]{1,0:T(8,128)(2,1)}) %all-gather.7.cloned.1.call-update) | async-done | bytes 2621456 | tf_op jit(solution)/shard_map/all_gather | solution.py:176
  89.2 4.4 %copy.49 = bf16[2,512,1280]{1,2,0:T(8,128)(2,1)} copy(bf16[2,512,1280]{2,1,0:T(8,128)(2,1)} %bitcast.170) | data formatting | bytes 5242880 | tf_op jit(solution)/shard_map/while | solution.py:47
  93.6 10.7 %while.7 = (s32[]{:T(128)}, f32[20,128]{1,0:T(8,128)S(1)}, f32[20,128]{1,0:T(8,128)S(1)}, f32[20,128]{1,0:T(8,128)S(1)}, bf16[2,512,1280]{1,2,0:T(8,128)(2,1)}, ...) while((s32[]{:T(128)}, f32[20,128]{1,0:T(8,128)S(1)}, ...), condition=%wide.region_8.9_spmd, body=%wide.region_4.8_spmd.sunk | while | flops 347348480 | bytes 24432744 | solution.py:47
  93.6 1.9 constant_dynamic-slice_fusion.10
  96.5 1.5 fusion.120
  98.9 1.9 constant_dynamic-slice_fusion.10
  101.9 1.5 fusion.120
  104.3 3.6 %fusion.51 = f32[20,128,64]{1,2,0:T(8,128)} fusion(bf16[256,20,64]{0,2,1:T(8,128)(2,1)} %bitcast.162, f32[20,128,256]{2,1,0:T(8,128)} %get-tuple-element.399, f32[20,128,256]{2,1,0:T(8,128)S(1)} %get-tuple-element.398, f32[20,128]{1,0:T(8,128)S(1)} %get-tuple-element.607), kind=kOutput, calls=%fused_computation.65 | convolution fusion | flops 86507520 | bytes 6563840 | tf_op jit(solution)/shard_map/while/body/eval_jaxpr/hqk,khe->hqe/dot_general | solution.py:67
  107.9 1.6 fusion.59
  109.5 30.4 %while.8 = (s32[]{:T(128)}, f32[20,128,64]{1,2,0:T(8,128)}, f32[20,128,64]{1,2,0:T(8,128)}, bf16[2,512,1280]{1,2,0:T(8,128)(2,1)}, bf16[128,20,64]{0,2,1:T(8,128...) while((s32[]{:T(128)}, f32[20,128,64]{1,2,0:T(8,128)}, ...), condition=%wide.region_10.11_spmd, body=%wide.region_9.10_spmd.sunk | while | flops 680591360 | bytes 29511784 | solution.py:93
  109.5 1.9 constant_dynamic-slice_fusion.11
  111.3 3.2 %fusion.129 = f32[20,512,128]{2,1,0:T(8,128)} fusion(bf16[512,20,64]{0,2,1:T(8,128)(2,1)S(1)} %bitcast.151, bf16[128,20,64]{0,2,1:T(8,128)(2,1)S(1)} %get-tuple-element.624), kind=kOutput, calls=%fused_computation.89.clone.1 | convolution fusion | flops 167772160 | bytes 6881280 | tf_op jit(solution)/shard_map/while/body/eval_jaxpr/qhe,khe->hqk/dot_general | solution.py:60
  114.6 5.4 %fusion.130 = f32[20,128,64]{1,2,0:T(8,128)} fusion(f32[20,128,64]{1,2,0:T(8,128)} %get-tuple-element.612, bf16[512,20,64]{0,2,1:T(8,128)(2,1)S(1)} %bitcast.152, f32[20,512,128]{2,1,0:T(8,128)} %fusion.129, bf16[512,20,64]{0,2,1:T(8,128)(2,1)S(1)} %bitcast.154, bf16[128,20,64]{0,2,1:T(8,128)(2,1)S(1)} %get-tuple-element.627, ...), kind=kOutput, calls=%fused_computation.22.clone.1 | convolution fusion | flops 340951040 | bytes 9512960 | tf_op jit(solution)/shard_map/while/body/eval_jaxpr/hqk,khe->hqe/dot_general | solution.py:67
  120.0 4.7 %fusion.131 = f32[20,128,64]{1,2,0:T(8,128)} fusion(f32[20,128,64]{1,2,0:T(8,128)} %get-tuple-element.613, bf16[512,20,64]{0,2,1:T(8,128)(2,1)S(1)} %bitcast.153, f32[20,512,128]{2,1,0:T(8,128)} %fusion.129, f32[20,128]{1,0:T(8,128)S(1)} %get-tuple-element.625), kind=kOutput, calls=%fused_computation.21.clone.1 | convolution fusion | flops 171868160 | bytes 7874560 | tf_op jit(solution)/shard_map/while/body/eval_jaxpr/hqk,khe->hqe/dot_general | solution.py:73
  124.6 1.9 constant_dynamic-slice_fusion.11
  126.5 3.2 %fusion.129 = f32[20,512,128]{2,1,0:T(8,128)} fusion(bf16[512,20,64]{0,2,1:T(8,128)(2,1)S(1)} %bitcast.151, bf16[128,20,64]{0,2,1:T(8,128)(2,1)S(1)} %get-tuple-element.624), kind=kOutput, calls=%fused_computation.89.clone.1 | convolution fusion | flops 167772160 | bytes 6881280 | tf_op jit(solution)/shard_map/while/body/eval_jaxpr/qhe,khe->hqk/dot_general | solution.py:60
  129.7 5.5 %fusion.130 = f32[20,128,64]{1,2,0:T(8,128)} fusion(f32[20,128,64]{1,2,0:T(8,128)} %get-tuple-element.612, bf16[512,20,64]{0,2,1:T(8,128)(2,1)S(1)} %bitcast.152, f32[20,512,128]{2,1,0:T(8,128)} %fusion.129, bf16[512,20,64]{0,2,1:T(8,128)(2,1)S(1)} %bitcast.154, bf16[128,20,64]{0,2,1:T(8,128)(2,1)S(1)} %get-tuple-element.627, ...), kind=kOutput, calls=%fused_computation.22.clone.1 | convolution fusion | flops 340951040 | bytes 9512960 | tf_op jit(solution)/shard_map/while/body/eval_jaxpr/hqk,khe->hqe/dot_general | solution.py:67
  135.2 4.6 %fusion.131 = f32[20,128,64]{1,2,0:T(8,128)} fusion(f32[20,128,64]{1,2,0:T(8,128)} %get-tuple-element.613, bf16[512,20,64]{0,2,1:T(8,128)(2,1)S(1)} %bitcast.153, f32[20,512,128]{2,1,0:T(8,128)} %fusion.129, f32[20,128]{1,0:T(8,128)S(1)} %get-tuple-element.625), kind=kOutput, calls=%fused_computation.21.clone.1 | convolution fusion | flops 171868160 | bytes 7874560 | tf_op jit(solution)/shard_map/while/body/eval_jaxpr/hqk,khe->hqe/dot_general | solution.py:73
  139.9 1.5 multiply_convert_fusion.12
  142.2 3.0 copy.52
  145.3 3.6 %reshape_reshape.8 = bf16[2,512,20,64]{1,0,3,2:T(2,128)(2,1)} reshape(bf16[1024,1280]{0,1:T(8,128)(2,1)S(1)} %copy.52) | data formatting | bytes 5242880 | tf_op jit(solution)/shard_map/reshape;reshape | solution.py:144
  148.9 4.1 %copy.53 = bf16[2,512,20,64]{1,3,2,0:T(8,128)(2,1)} copy(bf16[2,512,20,64]{1,0,3,2:T(2,128)(2,1)} %reshape_reshape.8) | data formatting | bytes 5242880
  152.9 13.9 %all_gather.31 = f32[1024,20]{0,1:T(8,128)S(1)} all-gather(f32[128,20]{0,1:T(8,128)S(1)} %bitcast.168), channel_id=1, replica_groups=mesh['grp'=4,'seq'=8] {'seq'}, dimensions={0}, use_global_device_ids=true | all-gather | bytes 92160 | tf_op jit(solution)/shard_map/all_gather | solution.py:197
  167.0 1.8 fusion.57
  168.8 2.1 convolution_multiply_fusion
  170.9 5.5 %reshape_reshape.9 = bf16[2,512,20,64]{1,0,3,2:T(2,128)(2,1)} reshape(bf16[1024,1280]{0,1:T(8,128)(2,1)} %all-gather.11.cloned.1.call-done) | data formatting | bytes 5242880 | tf_op jit(solution)/shard_map/reshape;reshape | solution.py:145
  176.5 2.3 copy.56
  178.8 13.9 %all_gather.33 = f32[1024,20]{0,1:T(8,128)S(1)} all-gather(f32[128,20]{0,1:T(8,128)S(1)} %bitcast.179), channel_id=1, replica_groups=mesh['grp'=4,'seq'=8] {'seq'}, dimensions={0}, use_global_device_ids=true | all-gather | bytes 92160 | tf_op jit(solution)/shard_map/all_gather | solution.py:198
  192.8 32.4 %while.9 = (s32[]{:T(128)}, f32[128,1280]{0,1:T(8,128)}, f32[128,1280]{0,1:T(8,128)}, bf16[2,512,20,64]{1,3,2,0:T(8,128)(2,1)}, bf16[128,1280]{0,1:T(8,128)(2,1)...) while((s32[]{:T(128)}, f32[128,1280]{0,1:T(8,128)}, ...), condition=%wide.region_12.13_spmd.clone, body=%wide.region_11.12_spmd.clone.sunk | while | flops 682393600 | bytes 48317608 | solution.py:140
  192.8 2.3 fusion.139
  195.2 3.6 %fusion.140 = f32[20,64,128]{2,1,0:T(8,128)S(1)} fusion(f32[20,512,128]{2,1,0:T(8,128)S(1)} %fusion.139, f32[20,512]{1,0:T(8,128)S(1)} %bitcast.166, bf16[2,512,20,64]{1,3,2,0:T(8,128)(2,1)S(1)} %get-tuple-element.657, s32[]{:T(128)S(6)} %copy.98), kind=kOutput, calls=%fused_computation.30.clone.1 | convolution fusion | flops 171704320 | bytes 7258116 | tf_op jit(solution)/shard_map/while/body/eval_jaxpr/hqk,qhe->khe/dot_general | solution.py:116
  198.8 7.6 %fusion.141 = f32[20,64,128]{2,1,0:T(8,128)} fusion(f32[20,512,128]{2,1,0:T(8,128)} %copy-done, f32[20,512]{1,0:T(8,128)S(1)} %bitcast.173, f32[20,512]{1,0:T(8,128)S(1)} %bitcast.167, bf16[128,20,64]{0,2,1:T(8,128)(2,1)} %bitcast.178, bf16[2,512,20,64]{1,3,2,0:T(8,128)(2,1)S(1)} %get-tuple-element.657, s32[]{:T(128)S(6)} %copy.98, ...), kind=kOutput, calls=%fused_computation.40.clone.1 | convolution fusion | flops 342261760 | bytes 8946688 | tf_op jit(solution)/shard_map/while/body/eval_jaxpr/hqk,qhe->khe/dot_general | solution.py:113
  206.4 2.4 bitcast_add_fusion.3
  208.8 2.3 fusion.139
  211.2 3.6 %fusion.140 = f32[20,64,128]{2,1,0:T(8,128)S(1)} fusion(f32[20,512,128]{2,1,0:T(8,128)S(1)} %fusion.139, f32[20,512]{1,0:T(8,128)S(1)} %bitcast.166, bf16[2,512,20,64]{1,3,2,0:T(8,128)(2,1)S(1)} %get-tuple-element.657, s32[]{:T(128)S(6)} %copy.98), kind=kOutput, calls=%fused_computation.30.clone.1 | convolution fusion | flops 171704320 | bytes 7258116 | tf_op jit(solution)/shard_map/while/body/eval_jaxpr/hqk,qhe->khe/dot_general | solution.py:116
  214.8 7.6 %fusion.141 = f32[20,64,128]{2,1,0:T(8,128)} fusion(f32[20,512,128]{2,1,0:T(8,128)} %copy-done, f32[20,512]{1,0:T(8,128)S(1)} %bitcast.173, f32[20,512]{1,0:T(8,128)S(1)} %bitcast.167, bf16[128,20,64]{0,2,1:T(8,128)(2,1)} %bitcast.178, bf16[2,512,20,64]{1,3,2,0:T(8,128)(2,1)S(1)} %get-tuple-element.657, s32[]{:T(128)S(6)} %copy.98, ...), kind=kOutput, calls=%fused_computation.40.clone.1 | convolution fusion | flops 342261760 | bytes 8946688 | tf_op jit(solution)/shard_map/while/body/eval_jaxpr/hqk,qhe->khe/dot_general | solution.py:113
  222.4 2.8 bitcast_add_fusion.3
  225.2 2.1 copy.59
  227.3 2.0 copy.60
  229.3 1.7 copy.61
  231.0 1.5 copy.62
  232.5 69.6 %all-reduce.2 = (bf16[256,1280]{1,0:T(8,128)(2,1)S(1)}, bf16[256,1280]{1,0:T(8,128)(2,1)S(1)}) all-reduce(f32[256,1280]{1,0:T(8,128)S(1)} %copy.61, f32[256,1280]{1,0:T(8,128)} %copy.62), channel_id=1, replica_groups=mesh['grp'=4,'seq'=8] {'grp','seq'}, use_global_device_ids=true, to_apply=%region_13.14 | all-reduce | flops 655360 | bytes 3932160 | tf_op jit(solution)/shard_map/psum | solution.py:214
  (75 shorter events, 14.5 us)
Async XLA Ops:
  7.2 6.5 %copy-start.7 = (bf16[128,1280]{1,0:T(8,128)(2,1)S(1)}, bf16[128,1280]{1,0:T(8,128)(2,1)}, u32[]{:S(2)}) copy-start(bf16[128,1280]{1,0:T(8,128)(2,1)} %param.14) | copy-start | bytes 983044
  7.2 7.4 %copy-start.8 = (bf16[128,1280]{1,0:T(8,128)(2,1)S(1)}, bf16[128,1280]{1,0:T(8,128)(2,1)}, u32[]{:S(2)}) copy-start(bf16[128,1280]{1,0:T(8,128)(2,1)} %param.15) | copy-start | bytes 983044
  7.2 6.2 %copy-start.9 = (bf16[128,1280]{1,0:T(8,128)(2,1)S(1)}, bf16[128,1280]{1,0:T(8,128)(2,1)}, u32[]{:S(2)}) copy-start(bf16[128,1280]{1,0:T(8,128)(2,1)} %param.13) | copy-start | bytes 983044
  7.2 8.3 %copy-start.12 = (bf16[32,1280]{1,0:T(8,128)(2,1)S(1)}, bf16[32,1280]{1,0:T(8,128)(2,1)}, u32[]{:S(2)}) copy-start(bf16[32,1280]{1,0:T(8,128)(2,1)} %param.17) | copy-start | bytes 245764
  7.2 56.4 %all-gather.5.cloned.1.call-start = ((), (), s32[]{:S(2)}) async-start(), calls=%async_computation | async-start | bytes 2949120 | tf_op jit(solution)/shard_map/all_gather | solution.py:175
  7.9 81.3 %all-gather.7.cloned.1.call-start = ((), (), s32[]{:S(2)}) async-start(), calls=%async_computation.1 | async-start | bytes 2949120 | tf_op jit(solution)/shard_map/all_gather | solution.py:176
  8.7 133.6 %all-gather.9.cloned.1.call-start = ((), (), s32[]{:S(2)}) async-start(), calls=%async_computation.2 | async-start | bytes 2949120 | tf_op jit(solution)/shard_map/all_gather | solution.py:201
  9.4 161.5 %all-gather.11.cloned.1.call-start = ((), (), s32[]{:S(2)}) async-start(), calls=%async_computation.3 | async-start | bytes 2949120 | tf_op jit(solution)/shard_map/all_gather | solution.py:202
  36.2 2.9 copy-start.13
  37.3 22.8 %copy-start.3 = (bf16[128,1280]{0,1:T(8,128)(2,1)S(1)}, bf16[128,1280]{0,1:T(8,128)(2,1)}, u32[]{:S(2)}) copy-start(bf16[128,1280]{0,1:T(8,128)(2,1)} %multiply_convert_fusion.13) | copy-start | bytes 983044
  39.0 68.9 %copy-start.1 = (f32[20,128,256]{2,1,0:T(8,128)}, f32[20,128,256]{2,1,0:T(8,128)S(1)}, u32[]{:S(2)}) copy-start(f32[20,128,256]{2,1,0:T(8,128)S(1)} %get-tuple-element.398) | copy-start | bytes 7864324
  104.3 64.4 %copy-start.10 = (f32[20,128]{1,0:T(8,128)}, f32[20,128]{1,0:T(8,128)S(1)}, u32[]{:S(2)}) copy-start(f32[20,128]{1,0:T(8,128)S(1)} %get-tuple-element.393) | copy-start | bytes 30724
  104.3 3.6 %copy-start.5 = (bf16[256,1280]{0,1:T(8,128)(2,1)S(1)}, bf16[256,1280]{0,1:T(8,128)(2,1)}, u32[]{:S(2)}) copy-start(bf16[256,1280]{0,1:T(8,128)(2,1)} %copy.45) | copy-start | bytes 1966084
  148.9 18.1 %copy-start.2 = (f32[20,128,256]{2,1,0:T(8,128)S(1)}, f32[20,128,256]{2,1,0:T(8,128)}, u32[]{:S(2)}) copy-start(f32[20,128,256]{2,1,0:T(8,128)} %copy-done.1) | copy-start | bytes 7864324
  166.9 1.9 copy-start.4
  176.4 2.3 copy-start.11
  195.1 3.6 %copy-start = (f32[20,512,128]{2,1,0:T(8,128)}, f32[20,512,128]{2,1,0:T(8,128)S(1)}, u32[]{:S(2)}) copy-start(f32[20,512,128]{2,1,0:T(8,128)S(1)} %fusion.139) | copy-start | bytes 15728644 | tf_op jit(solution)/shard_map/while
  211.1 3.6 %copy-start = (f32[20,512,128]{2,1,0:T(8,128)}, f32[20,512,128]{2,1,0:T(8,128)S(1)}, u32[]{:S(2)}) copy-start(f32[20,512,128]{2,1,0:T(8,128)S(1)} %fusion.139) | copy-start | bytes 15728644 | tf_op jit(solution)/shard_map/while
  225.2 5.8 %copy-start.6 = (f32[20,64,256]{2,1,0:T(8,128)S(1)}, f32[20,64,256]{2,1,0:T(8,128)}, u32[]{:S(2)}) copy-start(f32[20,64,256]{2,1,0:T(8,128)} %fusion.57) | copy-start | bytes 3932164
Sparse Core Ops, SparseCore 0:
  9.7 44.1 all-gather.4
  55.5 33.6 all-gather.6
  90.9 32.8 all-gather.8
  125.8 33.9 all-gather.10
where the time goes:
time: 311 us; the launch traced here: 309 us
  blocking collectives  137 us (44%)
  matrix products  72.9 us (23%)
  local copies, waits for them, and re-layouts  50.8 us (16%)
  waiting for transfers between devices  23 us (7%)
  between operations  14.7 us (5%)
  other arithmetic  10.5 us (3%)
    psum x1, blocking collectives, local(): summed = lax.psum((text_key_part, text_value_part), ('grp', 'seq'))  69.6 us
    all_gather x1, waiting for transfers between devices, local(): lax.all_gather(image_values, 'seq', axis=0, tiled=True)  20.9 us
    all_gather x1, blocking collectives, local(): lax.all_gather(text_keys, 'seq', axis=0, tiled=True)  20.7 us
    all_gather x1, blocking collectives, local(): lax.all_gather(text_values, 'seq', axis=0, tiled=True)  18.8 us
    dot_general x3, matrix products, key_block_terms(): jnp.einsum('hqk,qhe->khe', slopes, query_heads, preferred_element_type=jn...  17.4 us
    dot_general x3, matrix products, query_block_terms(): jnp.einsum('hqk,khe->hqe', (probabilities * products).astype(jnp.bfloat16...  14.5 us
    all_gather x1, blocking collectives, local(): lax.all_gather(grad_dot.T, 'seq', axis=0, tiled=True)  13.9 us
    all_gather x1, blocking collectives, local(): lax.all_gather(log_total.T, 'seq', axis=0, tiled=True)  13.9 us
  transfers between devices with their start and end apart: 4, of which 1 were waited for; matrix products, arithmetic and copies ran while one was open for 28% of the time, Pallas kernels for 0%

commit v1 on v0

--- a/solution.py
+++ b/solution.py
@@ -3,6 +3,8 @@
 import jax
 import jax.numpy as jnp
 from jax import lax
+from jax.experimental import pallas as pl
+from jax.experimental.pallas import tpu as pltpu
 from jax.sharding import PartitionSpec as P
 
 HEADS = 20
@@ -225,6 +227,391 @@
     )
 
 
+CHIPS = 4
+LANES = 128
+TILE = 256
+MESH = pl.DeviceIdType.MESH
+F32 = jnp.float32
+BF16 = jnp.bfloat16
+
+
+def low_lanes(rows):
+    return lax.broadcasted_iota(jnp.int32, (rows, LANES), 1) < HEAD_DIM
+
+
+def swapped(x):
+    return pltpu.roll(x.astype(F32), HEAD_DIM, 1)
+
+
+def pack_head(low, top, bottom):
+    mask = low_lanes(top.shape[0])
+    if low:
+        return jnp.where(mask, top.astype(F32), swapped(bottom))
+    return jnp.where(mask, swapped(top), bottom.astype(F32))
+
+
+def fused(
+    ranks, q_in, k_in, v_in, g_in, tk_in, tv_in,
+    dq_out, dk_out, dv_out, dtk_out, dtv_out,
+    send_a, send_c, recv_a, recv_c, sib_a, sib_c,
+    qs, gs, ks, vs, kt, dqs, acc, sib_acc,
+    osend_a, osend_c, orecv_a, orecv_c,
+    tterm_a, tterm_c, tz_a, tz_c, tzr_a, tzr_c,
+    in_s, in_r, sib_s, sib_r, acc_s, acc_r, out_s, out_r, grp_s, grp_r, tz_s, tz_r,
+):
+    rows = q_in.shape[0]
+    text = tk_in.shape[0]
+    images = ranks.shape[0]
+    grp = lax.axis_index("grp")
+    seq = lax.axis_index("seq")
+    z = seq // 2
+    core = seq % 2
+
+    def peer(step):
+        there = (z + step) % CHIPS
+        return there, {"seq": there * 2 + core}
+
+    def friend(step):
+        there = (grp + step) % images
+        return there, {"grp": there}
+
+    sibling = {"seq": z * 2 + 1 - core}
+
+    barrier = pltpu.get_barrier_semaphore()
+    for step in range(1, CHIPS):
+        pl.semaphore_signal(barrier, inc=1, device_id=peer(step)[1], device_id_type=MESH)
+    for step in range(1, images):
+        pl.semaphore_signal(barrier, inc=1, device_id=friend(step)[1], device_id_type=MESH)
+    pl.semaphore_signal(barrier, inc=1, device_id=sibling, device_id_type=MESH)
+
+    rank = ranks[grp].astype(F32)
+    advantage = (jnp.full((1, LANES), rank) - 0.5 * (images - 1)) / math.sqrt(
+        (images * images - 1) / 12.0
+    )
+
+    def cotangent(columns):
+        return (advantage * g_in[:, columns].astype(F32)).astype(BF16)
+
+    def part(t, pair_ref, single_ref):
+        return pair_ref.at[t] if t < 2 else single_ref
+
+    sizes = [(rows, text), (rows, text), (rows // 2, text // 2)]
+
+    def pack(t):
+        r, n = sizes[t]
+        dst = part(t, send_a, send_c)
+        for chip in range(CHIPS):
+            if t < 2:
+                cols = slice((2 * chip + t) * LANES, (2 * chip + t + 1) * LANES)
+                pieces = [
+                    q_in[:, cols], cotangent(cols), k_in[:, cols], tk_in[:, cols],
+                    v_in[:, cols], tv_in[:, cols],
+                ]
+            else:
+                cols = slice((8 + chip // 2) * LANES, (9 + chip // 2) * LANES)
+                whole = [
+                    q_in[:, cols], cotangent(cols), k_in[:, cols], tk_in[:, cols],
+                    v_in[:, cols], tv_in[:, cols],
+                ]
+                pieces = []
+                for x in whole:
+                    half = x.shape[0] // 2
+                    x = x.astype(F32)
+                    pieces.append(pack_head(chip % 2 == 0, x[:half], x[half:]).astype(BF16))
+            at = 0
+            for x in pieces:
+                dst[chip, at : at + x.shape[0], :] = x
+                at += x.shape[0]
+        part(t, recv_a, recv_c)[z] = dst[z]
+
+    def in_copy(t, step):
+        there, device = peer(step)
+        return pltpu.make_async_remote_copy(
+            src_ref=part(t, send_a, send_c).at[there],
+            dst_ref=part(t, recv_a, recv_c).at[z],
+            send_sem=in_s.at[t, step],
+            recv_sem=in_r.at[t, step],
+            device_id=device,
+            device_id_type=MESH,
+        )
+
+    def sib_copy(t):
+        r, n = sizes[t]
+        return pltpu.make_async_remote_copy(
+            src_ref=part(t, recv_a, recv_c).at[:, pl.ds(2 * r, 2 * r + 2 * n), :],
+            dst_ref=part(t, sib_a, sib_c),
+            send_sem=sib_s.at[t],
+            recv_sem=sib_r.at[t],
+            device_id=sibling,
+            device_id_type=MESH,
+        )
+
+    half_keys = CHIPS * (rows + text)
+    queries = CHIPS * rows
+
+    def acc_copy(t):
+        return pltpu.make_async_remote_copy(
+            src_ref=acc.at[t, :, pl.ds(half_keys, half_keys), :],
+            dst_ref=sib_acc.at[t],
+            send_sem=acc_s.at[t],
+            recv_sem=acc_r.at[t],
+            device_id=sibling,
+            device_id_type=MESH,
+        )
+
+    def out_copy(t, step):
+        there, device = peer(step)
+        return pltpu.make_async_remote_copy(
+            src_ref=part(t, osend_a, osend_c).at[there],
+            dst_ref=part(t, orecv_a, orecv_c).at[z],
+            send_sem=out_s.at[t, step],
+            recv_sem=out_r.at[t, step],
+            device_id=device,
+            device_id_type=MESH,
+        )
+
+    def grp_copy(t, step):
+        there, device = friend(step)
+        terms = part(t, tterm_a, tterm_c)
+        return pltpu.make_async_remote_copy(
+            src_ref=terms.at[grp],
+            dst_ref=terms.at[grp],
+            send_sem=grp_s.at[t, step],
+            recv_sem=grp_r.at[t, step],
+            device_id=device,
+            device_id_type=MESH,
+        )
+
+    def tz_copy(t, step):
+        there, device = peer(step)
+        return pltpu.make_async_remote_copy(
+            src_ref=part(t, tz_a, tz_c).at[there],
+            dst_ref=part(t, tzr_a, tzr_c).at[z],
+            send_sem=tz_s.at[t, step],
+            recv_sem=tz_r.at[t, step],
+            device_id=device,
+            device_id_type=MESH,
+        )
+
+    pack(0)
+    pl.semaphore_wait(barrier, CHIPS - 1 + images - 1 + 1)
+    for t in range(3):
+        if t > 0:
+            pack(t)
+        for step in range(1, CHIPS):
+            in_copy(t, step).start()
+
+    factor = HEAD_DIM ** (-0.5) * math.log2(math.e)
+
+    def gathered(x):
+        return x.reshape(x.shape[0] * x.shape[1], LANES)
+
+    def unpacked(x):
+        return jnp.concatenate([x.astype(F32), swapped(x)], 0).astype(BF16)
+
+    def load_queries(t):
+        r, n = sizes[t]
+        src = part(t, recv_a, recv_c)
+        for dst, at in ((qs, 0), (gs, r)):
+            x = gathered(src[:, at : at + r, :])
+            mask = low_lanes(queries)
+            if t < 2:
+                dst[0:queries] = jnp.where(mask, x, jnp.zeros_like(x))
+                dst[queries : 2 * queries] = jnp.where(mask, jnp.zeros_like(x), x)
+            else:
+                x = unpacked(x)
+                dst[0:queries] = jnp.where(mask, x, jnp.zeros_like(x))
+
+    def load_keys(t, source, base, at):
+        r, n = sizes[t]
+        for dst, shift in ((ks, 0), (vs, r + n)):
+            x = gathered(source[:, at + shift : at + shift + r + n, :])
+            if t == 2:
+                x = unpacked(x)
+            dst[base : base + half_keys] = x
+
+    def compute(t):
+        heads = 2 if t < 2 else 1
+        acc[t] = jnp.zeros(acc.shape[1:], F32)
+        kt[...] = ks[...].astype(F32).T.astype(BF16)
+
+        def body(i, carry):
+            place = pl.ds(pl.multiple_of(i * TILE, TILE), TILE)
+            q = qs[place, :]
+            g = gs[place, :]
+            nt = (((1,), (1,)), ((), ()))
+            s = lax.dot_general(ks[...], q, nt, preferred_element_type=F32)
+            dp = lax.dot_general(vs[...], g, nt, preferred_element_type=F32)
+            e = jnp.exp2((s - jnp.max(s, 0, keepdims=True)) * factor)
+            inverse = 1.0 / jnp.sum(e, 0, keepdims=True)
+            p = e * inverse
+            dot = jnp.sum(p * dp, 0, keepdims=True)
+            slopes = (p * (dp - dot)).astype(BF16)
+            acc[t, 0] += jnp.dot(slopes, q, preferred_element_type=F32)
+            acc[t, 1] += jnp.dot(p.astype(BF16), g, preferred_element_type=F32)
+            dqs[place, :] = jnp.dot(kt[...], slopes, preferred_element_type=F32).T
+            return carry
+
+        lax.fori_loop(0, heads * queries // TILE, body, 0)
+
+    scale = HEAD_DIM ** (-0.5)
+
+    def finish(t):
+        r, n = sizes[t]
+        dst = part(t, osend_a, osend_c)
+        mask = low_lanes(queries)
+        if t < 2:
+            x = jnp.where(mask, dqs[0:queries], dqs[queries : 2 * queries])
+        else:
+            x = pack_head(True, dqs[0 : queries // 2], dqs[queries // 2 : queries])
+        dst[:, 0:r, :] = (scale * x).astype(BF16).reshape(CHIPS, r, LANES)
+        acc_copy(t).wait_recv()
+        terms = part(t, tterm_a, tterm_c)
+        for which in range(2):
+            x = acc[t, which, 0:half_keys, :] + sib_acc[t, which]
+            if which == 0:
+                x = scale * x
+            if t == 2:
+                x = pack_head(True, x[: half_keys // 2], x[half_keys // 2 :])
+            x = x.reshape(CHIPS, r + n, LANES)
+            dst[:, (1 + which) * r : (2 + which) * r, :] = x[:, :r].astype(BF16)
+            terms[grp, :, which * n : (which + 1) * n, :] = x[:, r:]
+        for step in range(1, CHIPS):
+            out_copy(t, step).start()
+        for step in range(1, images):
+            grp_copy(t, step).start()
+        part(t, orecv_a, orecv_c)[z] = dst[z]
+
+    def finish_text(t):
+        terms = part(t, tterm_a, tterm_c)
+        for step in range(1, images):
+            grp_copy(t, step).wait_recv()
+        total = terms[0]
+        for image in range(1, images):
+            total = total + terms[image]
+        dst = part(t, tz_a, tz_c)
+        dst[...] = total.astype(BF16)
+        for step in range(1, CHIPS):
+            tz_copy(t, step).start()
+        part(t, tzr_a, tzr_c)[z] = dst[z]
+
+    def place_out(t):
+        r, n = sizes[t]
+        src = part(t, orecv_a, orecv_c)
+        for step in range(1, CHIPS):
+            out_copy(t, step).wait_recv()
+        for which, dst in ((0, dq_out), (1, dk_out), (2, dv_out)):
+            place(t, src, which * r, r, dst)
+
+    def place_text(t):
+        r, n = sizes[t]
+        src = part(t, tzr_a, tzr_c)
+        for step in range(1, CHIPS):
+            tz_copy(t, step).wait_recv()
+        for which, dst in ((0, dtk_out), (1, dtv_out)):
+            place(t, src, which * n, n, dst)
+
+    def place(t, src, at, r, dst):
+        if t < 2:
+            for chip in range(CHIPS):
+                cols = slice((2 * chip + t) * LANES, (2 * chip + t + 1) * LANES)
+                dst[:, cols] = src[chip, at : at + r, :]
+        else:
+            for pair in range(2):
+                cols = slice((8 + pair) * LANES, (9 + pair) * LANES)
+                low = src[2 * pair, at : at + r, :].astype(F32)
+                high = src[2 * pair + 1, at : at + r, :].astype(F32)
+                mask = low_lanes(r)
+                dst[0:r, cols] = jnp.where(mask, low, swapped(high)).astype(BF16)
+                dst[r : 2 * r, cols] = jnp.where(mask, swapped(low), high).astype(BF16)
+
+    for t in range(3):
+        r, n = sizes[t]
+        for step in range(1, CHIPS):
+            in_copy(t, step).wait_recv()
+        sib_copy(t).start()
+        load_queries(t)
+        load_keys(t, part(t, recv_a, recv_c), 0, 2 * r)
+        sib_copy(t).wait_recv()
+        load_keys(t, part(t, sib_a, sib_c), half_keys, 0)
+        compute(t)
+        acc_copy(t).start()
+        if t > 0:
+            finish_text(t - 1)
+        finish(t)
+    place_out(0)
+    place_text(0)
+    finish_text(2)
+    place_out(1)
+    place_text(1)
+    place_out(2)
+    place_text(2)
+    for t in range(3):
+        for step in range(1, CHIPS):
+            in_copy(t, step).wait_send()
+            out_copy(t, step).wait_send()
+            tz_copy(t, step).wait_send()
+        for step in range(1, images):
+            grp_copy(t, step).wait_send()
+        sib_copy(t).wait_send()
+        acc_copy(t).wait_send()
+
+
+def exchange(queries, image_keys, image_values, out_grad, text_keys, text_values, reward_ranks):
+    rows = queries.shape[0]
+    text = text_keys.shape[0]
+    images = reward_ranks.shape[0]
+    width = 4 * rows + 2 * text
+    keys = 2 * CHIPS * (rows + text)
+    asked = CHIPS * rows
+    like = lambda x: jax.ShapeDtypeStruct(x.shape, BF16)
+
+    def pair_and_single(count, n, dtype):
+        return [
+            pltpu.VMEM((2, count, n, LANES), dtype),
+            pltpu.VMEM((count, n // 2, LANES), dtype),
+        ]
+
+    def text_terms(n):
+        return [
+            pltpu.VMEM((2, images, CHIPS, n, LANES), F32),
+            pltpu.VMEM((images, CHIPS, n // 2, LANES), F32),
+        ]
+
+    dma = pltpu.SemaphoreType.DMA
+    return pl.pallas_call(
+        fused,
+        out_shape=[like(x) for x in (queries, image_keys, image_values, text_keys, text_values)],
+        in_specs=[pl.BlockSpec(memory_space=pltpu.SMEM)]
+        + [pl.BlockSpec(memory_space=pltpu.VMEM)] * 6,
+        out_specs=[pl.BlockSpec(memory_space=pltpu.VMEM)] * 5,
+        scratch_shapes=pair_and_single(CHIPS, width, BF16)
+        + pair_and_single(CHIPS, width, BF16)
+        + pair_and_single(CHIPS, 2 * rows + 2 * text, BF16)
+        + [
+            pltpu.VMEM((2 * asked, LANES), BF16),
+            pltpu.VMEM((2 * asked, LANES), BF16),
+            pltpu.VMEM((keys, LANES), BF16),
+            pltpu.VMEM((keys, LANES), BF16),
+            pltpu.VMEM((LANES, keys), BF16),
+            pltpu.VMEM((2 * asked, LANES), F32),
+            pltpu.VMEM((3, 2, keys, LANES), F32),
+            pltpu.VMEM((3, 2, keys // 2, LANES), F32),
+        ]
+        + pair_and_single(CHIPS, 3 * rows, BF16)
+        + pair_and_single(CHIPS, 3 * rows, BF16)
+        + text_terms(2 * text)
+        + pair_and_single(CHIPS, 2 * text, BF16)
+        + pair_and_single(CHIPS, 2 * text, BF16)
+        + [dma((3, CHIPS)), dma((3, CHIPS)), dma((3,)), dma((3,)), dma((3,)), dma((3,))]
+        + [dma((3, CHIPS)), dma((3, CHIPS)), dma((3, images)), dma((3, images))]
+        + [dma((3, CHIPS)), dma((3, CHIPS))],
+        compiler_params=pltpu.CompilerParams(
+            collective_id=0, has_side_effects=True, vmem_limit_bytes=56 * 1024 * 1024
+        ),
+    )(reward_ranks, queries, image_keys, image_values, out_grad, text_keys, text_values)
+
+
 def solution(mesh):
     in_specs = (
         P(("grp", "seq"), None),
@@ -242,4 +629,5 @@
         P("seq", None),
         P("seq", None),
     )
-    return jax.shard_map(local, mesh=mesh, in_specs=in_specs, out_specs=out_specs, check_vma=False)
+    body = exchange if mesh.shape["seq"] == 2 * CHIPS else local
+    return jax.shard_map(body, mesh=mesh, in_specs=in_specs, out_specs=out_specs, check_vma=False)

time: 311 us -> 75.7 us (0.24)
  blocking collectives: 137 us -> 0 us
  matrix products: 72.9 us -> 0 us
  Pallas kernels: 0 us -> 69.4 us
  local copies, waits for them, and re-layouts: 50.8 us -> 5.34 us
  waiting for transfers between devices: 23 us -> 0 us
  between operations: 14.7 us -> 0.66 us
  other arithmetic: 10.5 us -> 0 us
    dot_general x22 -> x0, matrix products: 72.9 us -> none  [the longest x3 17.4 us: key_block_terms(): jnp.einsum('hqk,qhe->khe', slopes, query_heads, preferred_element_type=jn...]
    psum x1 -> x0, blocking collectives: 69.6 us -> none  [local(): summed = lax.psum((text_key_part, text_value_part), ('grp', 'seq'))]
    pallas_call x0 -> x1, Pallas kernels: none -> 69.4 us  [exchange(): pl.pallas_call(fused, out_shape=[like(x) for x in (queries, image_keys, i...]
    all_gather x4 -> x0, blocking collectives: 67.3 us -> none  [the longest x1 20.7 us: local(): lax.all_gather(text_keys, 'seq', axis=0, tiled=True)]
    all_gather x4 -> x0, waiting for transfers between devices: 21 us -> none  [the longest x1 20.9 us: local(): lax.all_gather(image_values, 'seq', axis=0, tiled=True)]
    while x10 -> x0, local copies, waits for them, and re-layouts: 13.1 us -> none  [the longest x2 9.02 us: absorb(): lax.scan(absorb_one, running, (key_rows.reshape(count, width, -1), value_...]
    another operation x2 -> x0, local copies, waits for them, and re-layouts: 9.12 us -> none  [the longest x1 5.53 us: key_terms(): cotan_heads.reshape(count, width, HEADS, HEAD_DIM)]
    dynamic_slice x12 -> x0, local copies, waits for them, and re-layouts: 7.71 us -> none  [the longest x4 7.52 us: absorb(): lax.scan(absorb_one, running, (key_rows.reshape(count, width, -1), value_...]
  transfers between devices with their start and end apart: 4 -> 0, of which waited for: 1 -> 0; matrix products, arithmetic and copies ran while one was open for 28% -> 0% of each run, Pallas kernels for 0% -> 0%
where the time goes in v1:
time: 75.7 us; the launch traced here: 75.4 us
  Pallas kernels  69.4 us (92%)
  local copies, waits for them, and re-layouts  5.34 us (7%)
    pallas_call x1, Pallas kernels, exchange(): pl.pallas_call(fused, out_shape=[like(x) for x in (queries, image_keys, i...  69.4 us
    unnamed x13, local copies, waits for them, and re-layouts  5.34 us

profile of v1, /device:TPU:0, one launch (start us, length us, event | category | flops | bytes accessed | tf_op | source)
XLA Modules:
  0.0 75.4 jit_solution(16881149904015567206)
XLA Ops:
  0.6 69.4 %shard_map.110 = (bf16[128,1280]{1,0:T(8,128)(2,1)}, bf16[128,1280]{1,0:T(8,128)(2,1)}, bf16[128,1280]{1,0:T(8,128)(2,1)}, bf16[32,1280]{1,0:T(8,128)(2,1)}, bf16[32,1280]{1,0:T(8,128)(2,1)}) custom-call(s32[4]{0:T(128)} %ranks.1, bf16[128,1280]{1,0:T(8,128)(2,1)} %q_in.1, bf16[128,1280]{1,0:T(8,128)(2,1)} %k_in.1, bf16[128,1280]{1,0:T(8,128)(2,1)} %v_in.1, ...), custom_call_target="tpu_custom_call" | custom-call | tf_op jit(solution)/shard_map/pallas_call | solution.py:582
  70.1 0.0 copy-start.1
  70.1 1.8 %copy.17 = bf16[128,1280]{1,0:T(8,128)(2,1)} copy(bf16[128,1280]{1,0:T(8,128)(2,1)} %get-tuple-element.10) | data formatting | bytes 655360
  71.8 0.0 copy-done.1
  71.8 0.0 copy-start
  71.8 0.7 copy.18
  72.6 0.4 copy-done
  72.9 0.0 copy-start.3
  72.9 0.7 copy.19
  73.7 0.2 copy-done.3
  73.9 0.0 copy-start.2
  73.9 0.6 copy.20
  74.5 0.3 copy-done.2
  74.8 0.6 copy.21
Async XLA Ops:
  70.1 1.8 %copy-start.1 = (bf16[128,1280]{1,0:T(8,128)(2,1)S(1)}, bf16[128,1280]{1,0:T(8,128)(2,1)}, u32[]{:S(2)}) copy-start(bf16[128,1280]{1,0:T(8,128)(2,1)} %get-tuple-element.11) | copy-start | bytes 983044
  71.8 1.1 %copy-start = (bf16[128,1280]{1,0:T(8,128)(2,1)S(1)}, bf16[128,1280]{1,0:T(8,128)(2,1)}, u32[]{:S(2)}) copy-start(bf16[128,1280]{1,0:T(8,128)(2,1)} %get-tuple-element.12) | copy-start | bytes 983044
  72.9 0.9 %copy-start.3 = (bf16[32,1280]{1,0:T(8,128)(2,1)S(1)}, bf16[32,1280]{1,0:T(8,128)(2,1)}, u32[]{:S(2)}) copy-start(bf16[32,1280]{1,0:T(8,128)(2,1)} %get-tuple-element.13) | copy-start | bytes 245764
  73.9 0.9 %copy-start.2 = (bf16[32,1280]{1,0:T(8,128)(2,1)S(1)}, bf16[32,1280]{1,0:T(8,128)(2,1)}, u32[]{:S(2)}) copy-start(bf16[32,1280]{1,0:T(8,128)(2,1)} %get-tuple-element.14) | copy-start | bytes 245764

commit v2 on v1

--- a/solution.py
+++ b/solution.py
@@ -557,6 +557,15 @@
         acc_copy(t).wait_send()
 
 
+def write_out(*refs):
+    sems = refs[10]
+    copies = [pltpu.make_async_copy(refs[i], refs[5 + i], sems.at[i]) for i in range(5)]
+    for copy in copies:
+        copy.start()
+    for copy in copies:
+        copy.wait()
+
+
 def exchange(queries, image_keys, image_values, out_grad, text_keys, text_values, reward_ranks):
     rows = queries.shape[0]
     text = text_keys.shape[0]
@@ -579,7 +588,7 @@
         ]
 
     dma = pltpu.SemaphoreType.DMA
-    return pl.pallas_call(
+    results = pl.pallas_call(
         fused,
         out_shape=[like(x) for x in (queries, image_keys, image_values, text_keys, text_values)],
         in_specs=[pl.BlockSpec(memory_space=pltpu.SMEM)]
@@ -610,6 +619,13 @@
             collective_id=0, has_side_effects=True, vmem_limit_bytes=56 * 1024 * 1024
         ),
     )(reward_ranks, queries, image_keys, image_values, out_grad, text_keys, text_values)
+    return pl.pallas_call(
+        write_out,
+        out_shape=[like(x) for x in results],
+        in_specs=[pl.BlockSpec(memory_space=pltpu.VMEM)] * 5,
+        out_specs=[pl.BlockSpec(memory_space=pl.ANY)] * 5,
+        scratch_shapes=[dma((5,))],
+    )(*results)
 
 
 def solution(mesh):

time: 75.7 us -> 72.5 us (0.958)
  local copies, waits for them, and re-layouts: 5.34 us -> 0 us
  Pallas kernels: 69.4 us -> 71.7 us
    unnamed x13 -> x0, local copies, waits for them, and re-layouts: 5.34 us -> none
    pallas_call x0 -> x1, Pallas kernels: none -> 2.25 us  [exchange(): pl.pallas_call(write_out, out_shape=[like(x) for x in results], in_specs=...]
where the time goes in v2:
time: 72.5 us; the launch traced here: 72.3 us
  Pallas kernels  71.7 us (99%)
    pallas_call x1, Pallas kernels, exchange(): pl.pallas_call(fused, out_shape=[like(x) for x in (queries, image_keys, i...  69.4 us
    pallas_call x1, Pallas kernels, exchange(): pl.pallas_call(write_out, out_shape=[like(x) for x in results], in_specs=...  2.25 us

profile of v2, /device:TPU:0, one launch (start us, length us, event | category | flops | bytes accessed | tf_op | source)
XLA Modules:
  0.0 72.3 jit_solution(16830418962986131969)
XLA Ops:
  0.6 69.4 %shard_map.110 = (bf16[128,1280]{1,0:T(8,128)(2,1)}, bf16[128,1280]{1,0:T(8,128)(2,1)}, bf16[128,1280]{1,0:T(8,128)(2,1)}, bf16[32,1280]{1,0:T(8,128)(2,1)}, bf16[32,1280]{1,0:T(8,128)(2,1)}) custom-call(s32[4]{0:T(128)} %ranks.1, bf16[128,1280]{1,0:T(8,128)(2,1)} %q_in.1, bf16[128,1280]{1,0:T(8,128)(2,1)} %k_in.1, bf16[128,1280]{1,0:T(8,128)(2,1)} %v_in.1, ...), custom_call_target="tpu_custom_call" | custom-call | tf_op jit(solution)/shard_map/pallas_call | solution.py:591
  70.1 2.3 %shard_map.111 = (bf16[128,1280]{1,0:T(8,128)(2,1)}, bf16[128,1280]{1,0:T(8,128)(2,1)}, bf16[128,1280]{1,0:T(8,128)(2,1)}, bf16[32,1280]{1,0:T(8,128)(2,1)}, bf16[32,1280]{1,0:T(8,128)(2,1)}) custom-call(bf16[128,1280]{1,0:T(8,128)(2,1)} %get-tuple-element.10.refs_0_, bf16[128,1280]{1,0:T(8,128)(2,1)} %get-tuple-element.11.refs_1_, ...), custom_call_target="tpu_custom_call" | custom-call | tf_op jit(solution)/shard_map/pallas_call | solution.py:622

commit v3 on v2

--- a/solution.py
+++ b/solution.py
@@ -256,8 +256,8 @@
     send_a, send_c, recv_a, recv_c, sib_a, sib_c,
     qs, gs, ks, vs, kt, dqs, acc, sib_acc,
     osend_a, osend_c, orecv_a, orecv_c,
-    tterm_a, tterm_c, tz_a, tz_c, tzr_a, tzr_c,
-    in_s, in_r, sib_s, sib_r, acc_s, acc_r, out_s, out_r, grp_s, grp_r, tz_s, tz_r,
+    tsend, tterm_a, tterm_c, tz_a, tz_c, tshare, tzr_c,
+    in_s, in_r, sib_s, sib_r, acc_s, acc_r, out_s, out_r, grp_s, grp_r, tz_s, tz_r, share_s, share_r,
 ):
     rows = q_in.shape[0]
     text = tk_in.shape[0]
@@ -370,23 +370,41 @@
             device_id_type=MESH,
         )
 
+    share = 2 * text // images
+
     def grp_copy(t, step):
         there, device = friend(step)
-        terms = part(t, tterm_a, tterm_c)
+        if t < 2:
+            src = tsend.at[t, there]
+            dst = tterm_a.at[t, grp]
+        else:
+            src = tterm_c.at[grp]
+            dst = tterm_c.at[grp]
         return pltpu.make_async_remote_copy(
-            src_ref=terms.at[grp],
-            dst_ref=terms.at[grp],
+            src_ref=src,
+            dst_ref=dst,
             send_sem=grp_s.at[t, step],
             recv_sem=grp_r.at[t, step],
             device_id=device,
             device_id_type=MESH,
         )
 
+    def share_copy(t, step):
+        there, device = friend(step)
+        return pltpu.make_async_remote_copy(
+            src_ref=tshare.at[t, grp],
+            dst_ref=tshare.at[t, grp],
+            send_sem=share_s.at[t, step],
+            recv_sem=share_r.at[t, step],
+            device_id=device,
+            device_id_type=MESH,
+        )
+
     def tz_copy(t, step):
         there, device = peer(step)
         return pltpu.make_async_remote_copy(
-            src_ref=part(t, tz_a, tz_c).at[there],
-            dst_ref=part(t, tzr_a, tzr_c).at[z],
+            src_ref=(tz_a.at[t] if t < 2 else tz_c).at[there],
+            dst_ref=tshare.at[t, grp, z] if t < 2 else tzr_c.at[z],
             send_sem=tz_s.at[t, step],
             recv_sem=tz_r.at[t, step],
             device_id=device,
@@ -466,7 +484,6 @@
             x = pack_head(True, dqs[0 : queries // 2], dqs[queries // 2 : queries])
         dst[:, 0:r, :] = (scale * x).astype(BF16).reshape(CHIPS, r, LANES)
         acc_copy(t).wait_recv()
-        terms = part(t, tterm_a, tterm_c)
         for which in range(2):
             x = acc[t, which, 0:half_keys, :] + sib_acc[t, which]
             if which == 0:
@@ -475,11 +492,18 @@
                 x = pack_head(True, x[: half_keys // 2], x[half_keys // 2 :])
             x = x.reshape(CHIPS, r + n, LANES)
             dst[:, (1 + which) * r : (2 + which) * r, :] = x[:, :r].astype(BF16)
-            terms[grp, :, which * n : (which + 1) * n, :] = x[:, r:]
+            if t < 2:
+                half = images // 2
+                for j in range(half):
+                    tsend[t, which * half + j] = x[:, r + j * share : r + (j + 1) * share]
+            else:
+                tterm_c[grp, :, which * n : (which + 1) * n, :] = x[:, r:]
         for step in range(1, CHIPS):
             out_copy(t, step).start()
         for step in range(1, images):
             grp_copy(t, step).start()
+        if t < 2:
+            tterm_a[t, grp] = tsend[t, grp]
         part(t, orecv_a, orecv_c)[z] = dst[z]
 
     def finish_text(t):
@@ -493,7 +517,16 @@
         dst[...] = total.astype(BF16)
         for step in range(1, CHIPS):
             tz_copy(t, step).start()
-        part(t, tzr_a, tzr_c)[z] = dst[z]
+        if t < 2:
+            tshare[t, grp, z] = dst[z]
+        else:
+            tzr_c[z] = dst[z]
+
+    def share_text(t):
+        for step in range(1, CHIPS):
+            tz_copy(t, step).wait_recv()
+        for step in range(1, images):
+            share_copy(t, step).start()
 
     def place_out(t):
         r, n = sizes[t]
@@ -505,11 +538,20 @@
 
     def place_text(t):
         r, n = sizes[t]
-        src = part(t, tzr_a, tzr_c)
+        if t < 2:
+            for step in range(1, images):
+                share_copy(t, step).wait_recv()
+            half = images // 2
+            for which, dst in ((0, dtk_out), (1, dtv_out)):
+                for chip in range(CHIPS):
+                    cols = slice((2 * chip + t) * LANES, (2 * chip + t + 1) * LANES)
+                    for j in range(half):
+                        dst[j * share : (j + 1) * share, cols] = tshare[t, which * half + j, chip]
+            return
         for step in range(1, CHIPS):
             tz_copy(t, step).wait_recv()
         for which, dst in ((0, dtk_out), (1, dtv_out)):
-            place(t, src, which * n, n, dst)
+            place(t, tzr_c, which * n, n, dst)
 
     def place(t, src, at, r, dst):
         if t < 2:
@@ -539,9 +581,11 @@
         if t > 0:
             finish_text(t - 1)
         finish(t)
+    share_text(0)
+    finish_text(2)
+    share_text(1)
     place_out(0)
     place_text(0)
-    finish_text(2)
     place_out(1)
     place_text(1)
     place_out(2)
@@ -553,6 +597,8 @@
             tz_copy(t, step).wait_send()
         for step in range(1, images):
             grp_copy(t, step).wait_send()
+            if t < 2:
+                share_copy(t, step).wait_send()
         sib_copy(t).wait_send()
         acc_copy(t).wait_send()
 
@@ -583,7 +629,8 @@
 
     def text_terms(n):
         return [
-            pltpu.VMEM((2, images, CHIPS, n, LANES), F32),
+            pltpu.VMEM((2, images, CHIPS, n // images, LANES), F32),
+            pltpu.VMEM((2, images, CHIPS, n // images, LANES), F32),
             pltpu.VMEM((images, CHIPS, n // 2, LANES), F32),
         ]
 
@@ -610,11 +657,15 @@
         + pair_and_single(CHIPS, 3 * rows, BF16)
         + pair_and_single(CHIPS, 3 * rows, BF16)
         + text_terms(2 * text)
-        + pair_and_single(CHIPS, 2 * text, BF16)
-        + pair_and_single(CHIPS, 2 * text, BF16)
+        + [
+            pltpu.VMEM((2, CHIPS, 2 * text // images, LANES), BF16),
+            pltpu.VMEM((CHIPS, text, LANES), BF16),
+            pltpu.VMEM((2, images, CHIPS, 2 * text // images, LANES), BF16),
+            pltpu.VMEM((CHIPS, text, LANES), BF16),
+        ]
         + [dma((3, CHIPS)), dma((3, CHIPS)), dma((3,)), dma((3,)), dma((3,)), dma((3,))]
         + [dma((3, CHIPS)), dma((3, CHIPS)), dma((3, images)), dma((3, images))]
-        + [dma((3, CHIPS)), dma((3, CHIPS))],
+        + [dma((3, CHIPS)), dma((3, CHIPS)), dma((2, images)), dma((2, images))],
         compiler_params=pltpu.CompilerParams(
             collective_id=0, has_side_effects=True, vmem_limit_bytes=56 * 1024 * 1024
         ),

time: 72.5 us -> 72.7 us (level)
  no operation moved by 1% of the time
where the time goes in v3:
time: 72.7 us; the launch traced here: 72.5 us
  Pallas kernels  71.8 us (99%)
    pallas_call x1, Pallas kernels, exchange(): pl.pallas_call(fused, out_shape=[like(x) for x in (queries, image_keys, i...  69.6 us
    pallas_call x1, Pallas kernels, exchange(): pl.pallas_call(write_out, out_shape=[like(x) for x in results], in_specs=...  2.25 us

profile of v3, /device:TPU:0, one launch (start us, length us, event | category | flops | bytes accessed | tf_op | source)
XLA Modules:
  0.0 72.5 jit_solution(13812620627606890673)
XLA Ops:
  0.6 69.6 %shard_map.110 = (bf16[128,1280]{1,0:T(8,128)(2,1)}, bf16[128,1280]{1,0:T(8,128)(2,1)}, bf16[128,1280]{1,0:T(8,128)(2,1)}, bf16[32,1280]{1,0:T(8,128)(2,1)}, bf16[32,1280]{1,0:T(8,128)(2,1)}) custom-call(s32[4]{0:T(128)} %ranks.1, bf16[128,1280]{1,0:T(8,128)(2,1)} %q_in.1, bf16[128,1280]{1,0:T(8,128)(2,1)} %k_in.1, bf16[128,1280]{1,0:T(8,128)(2,1)} %v_in.1, ...), custom_call_target="tpu_custom_call" | custom-call | tf_op jit(solution)/shard_map/pallas_call | solution.py:638
  70.2 2.3 %shard_map.111 = (bf16[128,1280]{1,0:T(8,128)(2,1)}, bf16[128,1280]{1,0:T(8,128)(2,1)}, bf16[128,1280]{1,0:T(8,128)(2,1)}, bf16[32,1280]{1,0:T(8,128)(2,1)}, bf16[32,1280]{1,0:T(8,128)(2,1)}) custom-call(bf16[128,1280]{1,0:T(8,128)(2,1)} %get-tuple-element.10.refs_0_, bf16[128,1280]{1,0:T(8,128)(2,1)} %get-tuple-element.11.refs_1_, ...), custom_call_target="tpu_custom_call" | custom-call | tf_op jit(solution)/shard_map/pallas_call | solution.py:673

commit v4 on v3

--- a/solution.py
+++ b/solution.py
@@ -256,8 +256,8 @@
     send_a, send_c, recv_a, recv_c, sib_a, sib_c,
     qs, gs, ks, vs, kt, dqs, acc, sib_acc,
     osend_a, osend_c, orecv_a, orecv_c,
-    tsend, tterm_a, tterm_c, tz_a, tz_c, tshare, tzr_c,
-    in_s, in_r, sib_s, sib_r, acc_s, acc_r, out_s, out_r, grp_s, grp_r, tz_s, tz_r, share_s, share_r,
+    tsend, tterm_a, tterm_c, tz_a, tz_c, tshare, tzr_c, tpiece, tgot,
+    in_s, in_r, sib_s, sib_r, acc_s, acc_r, out_s, out_r, grp_s, grp_r, tz_s, tz_r, share_s, share_r, ti_s, ti_r, tf_s, tf_r,
 ):
     rows = q_in.shape[0]
     text = tk_in.shape[0]
@@ -303,15 +303,12 @@
         for chip in range(CHIPS):
             if t < 2:
                 cols = slice((2 * chip + t) * LANES, (2 * chip + t + 1) * LANES)
-                pieces = [
-                    q_in[:, cols], cotangent(cols), k_in[:, cols], tk_in[:, cols],
-                    v_in[:, cols], tv_in[:, cols],
-                ]
+                pieces = [q_in[:, cols], cotangent(cols), k_in[:, cols], v_in[:, cols]]
             else:
                 cols = slice((8 + chip // 2) * LANES, (9 + chip // 2) * LANES)
                 whole = [
-                    q_in[:, cols], cotangent(cols), k_in[:, cols], tk_in[:, cols],
-                    v_in[:, cols], tv_in[:, cols],
+                    q_in[:, cols], cotangent(cols), k_in[:, cols], v_in[:, cols],
+                    tk_in[:, cols], tv_in[:, cols],
                 ]
                 pieces = []
                 for x in whole:
@@ -322,10 +319,57 @@
             for x in pieces:
                 dst[chip, at : at + x.shape[0], :] = x
                 at += x.shape[0]
-        part(t, recv_a, recv_c)[z] = dst[z]
+        if t < 2:
+            recv_a[t, z, 0 : 4 * rows, :] = send_a[t, z, 0 : 4 * rows, :]
+        else:
+            recv_c[z] = send_c[z]
+
+    share = 2 * text // images
+
+    def pack_text(t):
+        for chip in range(CHIPS):
+            cols = slice((2 * chip + t) * LANES, (2 * chip + t + 1) * LANES)
+            for which, x in ((0, tk_in), (1, tv_in)):
+                for j in range(images // 2):
+                    tpiece[t, which * (images // 2) + j, chip] = x[
+                        j * share : (j + 1) * share, cols
+                    ]
+        tgot[t, grp, z] = tpiece[t, grp, z]
+
+    def text_copy(t, step):
+        there, device = peer(step)
+        return pltpu.make_async_remote_copy(
+            src_ref=tpiece.at[t, grp, there],
+            dst_ref=tgot.at[t, grp, z],
+            send_sem=ti_s.at[t, step],
+            recv_sem=ti_r.at[t, step],
+            device_id=device,
+            device_id_type=MESH,
+        )
+
+    def spread_copy(t, step):
+        there, device = friend(step)
+        return pltpu.make_async_remote_copy(
+            src_ref=tgot.at[t, grp],
+            dst_ref=tgot.at[t, grp],
+            send_sem=tf_s.at[t, step],
+            recv_sem=tf_r.at[t, step],
+            device_id=device,
+            device_id_type=MESH,
+        )
 
     def in_copy(t, step):
         there, device = peer(step)
+        if t < 2:
+            image_rows = pl.ds(0, 4 * rows)
+            return pltpu.make_async_remote_copy(
+                src_ref=send_a.at[t, there, image_rows, :],
+                dst_ref=recv_a.at[t, z, image_rows, :],
+                send_sem=in_s.at[t, step],
+                recv_sem=in_r.at[t, step],
+                device_id=device,
+                device_id_type=MESH,
+            )
         return pltpu.make_async_remote_copy(
             src_ref=part(t, send_a, send_c).at[there],
             dst_ref=part(t, recv_a, recv_c).at[z],
@@ -370,8 +414,6 @@
             device_id_type=MESH,
         )
 
-    share = 2 * text // images
-
     def grp_copy(t, step):
         there, device = friend(step)
         if t < 2:
@@ -411,13 +453,24 @@
             device_id_type=MESH,
         )
 
+    for t in range(2):
+        pack_text(t)
     pack(0)
     pl.semaphore_wait(barrier, CHIPS - 1 + images - 1 + 1)
+    for t in range(2):
+        for step in range(1, CHIPS):
+            text_copy(t, step).start()
     for t in range(3):
         if t > 0:
             pack(t)
         for step in range(1, CHIPS):
             in_copy(t, step).start()
+
+    for t in range(2):
+        for step in range(1, CHIPS):
+            text_copy(t, step).wait_recv()
+        for step in range(1, images):
+            spread_copy(t, step).start()
 
     factor = HEAD_DIM ** (-0.5) * math.log2(math.e)
 
@@ -442,8 +495,16 @@
 
     def load_keys(t, source, base, at):
         r, n = sizes[t]
-        for dst, shift in ((ks, 0), (vs, r + n)):
-            x = gathered(source[:, at + shift : at + shift + r + n, :])
+        for dst, shift, text_at in ((ks, 0, 2 * r), (vs, r, 2 * r + n)):
+            x = gathered(
+                jnp.concatenate(
+                    [
+                        source[:, at + shift : at + shift + r, :],
+                        source[:, at + text_at : at + text_at + n, :],
+                    ],
+                    1,
+                )
+            )
             if t == 2:
                 x = unpacked(x)
             dst[base : base + half_keys] = x
@@ -571,6 +632,12 @@
         r, n = sizes[t]
         for step in range(1, CHIPS):
             in_copy(t, step).wait_recv()
+        if t < 2:
+            for step in range(1, images):
+                spread_copy(t, step).wait_recv()
+            for j in range(images):
+                place_at = 4 * rows + j * share
+                recv_a[t, :, place_at : place_at + share, :] = tgot[t, j]
         sib_copy(t).start()
         load_queries(t)
         load_keys(t, part(t, recv_a, recv_c), 0, 2 * r)
@@ -581,8 +648,8 @@
         if t > 0:
             finish_text(t - 1)
         finish(t)
+    finish_text(2)
     share_text(0)
-    finish_text(2)
     share_text(1)
     place_out(0)
     place_text(0)
@@ -593,12 +660,15 @@
     for t in range(3):
         for step in range(1, CHIPS):
             in_copy(t, step).wait_send()
+            if t < 2:
+                text_copy(t, step).wait_send()
             out_copy(t, step).wait_send()
             tz_copy(t, step).wait_send()
         for step in range(1, images):
             grp_copy(t, step).wait_send()
             if t < 2:
                 share_copy(t, step).wait_send()
+                spread_copy(t, step).wait_send()
         sib_copy(t).wait_send()
         acc_copy(t).wait_send()
 
@@ -662,10 +732,13 @@
             pltpu.VMEM((CHIPS, text, LANES), BF16),
             pltpu.VMEM((2, images, CHIPS, 2 * text // images, LANES), BF16),
             pltpu.VMEM((CHIPS, text, LANES), BF16),
+            pltpu.VMEM((2, images, CHIPS, 2 * text // images, LANES), BF16),
+            pltpu.VMEM((2, images, CHIPS, 2 * text // images, LANES), BF16),
         ]
         + [dma((3, CHIPS)), dma((3, CHIPS)), dma((3,)), dma((3,)), dma((3,)), dma((3,))]
         + [dma((3, CHIPS)), dma((3, CHIPS)), dma((3, images)), dma((3, images))]
-        + [dma((3, CHIPS)), dma((3, CHIPS)), dma((2, images)), dma((2, images))],
+        + [dma((3, CHIPS)), dma((3, CHIPS)), dma((2, images)), dma((2, images))]
+        + [dma((2, CHIPS)), dma((2, CHIPS)), dma((2, images)), dma((2, images))],
         compiler_params=pltpu.CompilerParams(
             collective_id=0, has_side_effects=True, vmem_limit_bytes=56 * 1024 * 1024
         ),

time: 72.7 us -> 68.7 us (0.945)
  Pallas kernels: 71.8 us -> 67.9 us
    pallas_call x1, Pallas kernels: 69.6 us -> 65.6 us  [exchange(): pl.pallas_call(fused, out_shape=[like(x) for x in (queries, image_keys, i...]
where the time goes in v4:
time: 68.7 us; the launch traced here: 68.5 us
  Pallas kernels  67.9 us (99%)
    pallas_call x1, Pallas kernels, exchange(): pl.pallas_call(fused, out_shape=[like(x) for x in (queries, image_keys, i...  65.6 us
    pallas_call x1, Pallas kernels, exchange(): pl.pallas_call(write_out, out_shape=[like(x) for x in results], in_specs=...  2.25 us

profile of v4, /device:TPU:0, one launch (start us, length us, event | category | flops | bytes accessed | tf_op | source)
XLA Modules:
  0.0 68.5 jit_solution(15207138243538208590)
XLA Ops:
  0.6 65.6 %shard_map.110 = (bf16[128,1280]{1,0:T(8,128)(2,1)}, bf16[128,1280]{1,0:T(8,128)(2,1)}, bf16[128,1280]{1,0:T(8,128)(2,1)}, bf16[32,1280]{1,0:T(8,128)(2,1)}, bf16[32,1280]{1,0:T(8,128)(2,1)}) custom-call(s32[4]{0:T(128)} %ranks.1, bf16[128,1280]{1,0:T(8,128)(2,1)} %q_in.1, bf16[128,1280]{1,0:T(8,128)(2,1)} %k_in.1, bf16[128,1280]{1,0:T(8,128)(2,1)} %v_in.1, ...), custom_call_target="tpu_custom_call" | custom-call | tf_op jit(solution)/shard_map/pallas_call | solution.py:708
  66.3 2.3 %shard_map.111 = (bf16[128,1280]{1,0:T(8,128)(2,1)}, bf16[128,1280]{1,0:T(8,128)(2,1)}, bf16[128,1280]{1,0:T(8,128)(2,1)}, bf16[32,1280]{1,0:T(8,128)(2,1)}, bf16[32,1280]{1,0:T(8,128)(2,1)}) custom-call(bf16[128,1280]{1,0:T(8,128)(2,1)} %get-tuple-element.10.refs_0_, bf16[128,1280]{1,0:T(8,128)(2,1)} %get-tuple-element.11.refs_1_, ...), custom_call_target="tpu_custom_call" | custom-call | tf_op jit(solution)/shard_map/pallas_call | solution.py:746

commit v5 on v4

--- a/solution.py
+++ b/solution.py
@@ -394,9 +394,10 @@
     queries = CHIPS * rows
 
     def acc_copy(t):
-        return pltpu.make_async_remote_copy(
-            src_ref=acc.at[t, :, pl.ds(half_keys, half_keys), :],
-            dst_ref=sib_acc.at[t],
+        count = half_keys if t < 2 else half_keys // 2
+        return pltpu.make_async_remote_copy(
+            src_ref=acc.at[t, :, pl.ds(half_keys, count), :],
+            dst_ref=sib_acc.at[t, :, pl.ds(0, count), :],
             send_sem=acc_s.at[t],
             recv_sem=acc_r.at[t],
             device_id=sibling,
@@ -546,11 +547,14 @@
         dst[:, 0:r, :] = (scale * x).astype(BF16).reshape(CHIPS, r, LANES)
         acc_copy(t).wait_recv()
         for which in range(2):
-            x = acc[t, which, 0:half_keys, :] + sib_acc[t, which]
+            x = acc[t, which, 0:half_keys, :]
+            if t == 2:
+                x = pack_head(True, x[: half_keys // 2], x[half_keys // 2 :])
+                x = x + sib_acc[t, which, 0 : half_keys // 2, :]
+            else:
+                x = x + sib_acc[t, which]
             if which == 0:
                 x = scale * x
-            if t == 2:
-                x = pack_head(True, x[: half_keys // 2], x[half_keys // 2 :])
             x = x.reshape(CHIPS, r + n, LANES)
             dst[:, (1 + which) * r : (2 + which) * r, :] = x[:, :r].astype(BF16)
             if t < 2:
@@ -644,6 +648,12 @@
         sib_copy(t).wait_recv()
         load_keys(t, part(t, sib_a, sib_c), half_keys, 0)
         compute(t)
+        if t == 2:
+            middle = half_keys + half_keys // 2
+            for which in range(2):
+                acc[t, which, half_keys:middle, :] = pack_head(
+                    True, acc[t, which, half_keys:middle, :], acc[t, which, middle:, :]
+                )
         acc_copy(t).start()
         if t > 0:
             finish_text(t - 1)

time: 68.7 us -> 68.4 us (level)
  no operation moved by 1% of the time
where the time goes in v5:
time: 68.4 us; the launch traced here: 68.2 us
  Pallas kernels  67.6 us (99%)
    pallas_call x1, Pallas kernels, exchange(): pl.pallas_call(fused, out_shape=[like(x) for x in (queries, image_keys, i...  65.3 us
    pallas_call x1, Pallas kernels, exchange(): pl.pallas_call(write_out, out_shape=[like(x) for x in results], in_specs=...  2.25 us

profile of v5, /device:TPU:0, one launch (start us, length us, event | category | flops | bytes accessed | tf_op | source)
XLA Modules:
  0.0 68.2 jit_solution(12313673023962092723)
XLA Ops:
  0.6 65.3 %shard_map.110 = (bf16[128,1280]{1,0:T(8,128)(2,1)}, bf16[128,1280]{1,0:T(8,128)(2,1)}, bf16[128,1280]{1,0:T(8,128)(2,1)}, bf16[32,1280]{1,0:T(8,128)(2,1)}, bf16[32,1280]{1,0:T(8,128)(2,1)}) custom-call(s32[4]{0:T(128)} %ranks.1, bf16[128,1280]{1,0:T(8,128)(2,1)} %q_in.1, bf16[128,1280]{1,0:T(8,128)(2,1)} %k_in.1, bf16[128,1280]{1,0:T(8,128)(2,1)} %v_in.1, ...), custom_call_target="tpu_custom_call" | custom-call | tf_op jit(solution)/shard_map/pallas_call | solution.py:718
  65.9 2.3 %shard_map.111 = (bf16[128,1280]{1,0:T(8,128)(2,1)}, bf16[128,1280]{1,0:T(8,128)(2,1)}, bf16[128,1280]{1,0:T(8,128)(2,1)}, bf16[32,1280]{1,0:T(8,128)(2,1)}, bf16[32,1280]{1,0:T(8,128)(2,1)}) custom-call(bf16[128,1280]{1,0:T(8,128)(2,1)} %get-tuple-element.10.refs_0_, bf16[128,1280]{1,0:T(8,128)(2,1)} %get-tuple-element.11.refs_1_, ...), custom_call_target="tpu_custom_call" | custom-call | tf_op jit(solution)/shard_map/pallas_call | solution.py:756
